TPU v7x, 32 devices: a whole 2x2x4 slice. The times are simulated.
32 devices in a mesh: row: 4 (over y, x), col: 8 (over z, core).
Axes of the slice: x: 2, y: 2, z: 4, core: 2. Of those that a mesh axis runs over, the one named last changes fastest.
Arguments:
- density: float32 [6144, 6144], P('row', 'col'), may hold values from -1 to 1, as said below
- response: float32 [6144, 6144], P('row', 'col'), may hold values from -1 to 1, as said below
- density_mask: int32 [48, 48], replicated, may hold values from 0 to 1, as said below
- response_mask: int32 [48, 48], replicated, may hold values from 0 to 1, as said below
- branch: int32 [48], replicated, may hold values from 0 to 1
Outputs:
- new_density: float32 [6144, 6144], P('row', 'col')
- new_response: float32 [6144, 6144], P('row', 'col')
Inputs may be any that keep to these rules, and one draw needn't show every extreme that they name: `density`: symmetric: equal to its own transpose. `response`: symmetric: equal to its own transpose. `density_mask`: symmetric, with ones on the diagonal. `response_mask`: symmetric, with ones on the diagonal.
All inputs are finite; a program needn't handle non-finite values.
Results may differ from a plain program's by a relative error of at most 0.000067.
Values sent between devices are 32-bit elements; how exact they have to be, the bound alone decides.
A program may use at most 192 MiB of HBM per device.

v0:
```python
import jax
import jax.numpy as jnp
from jax import lax
from jax.sharding import PartitionSpec as P

BLOCK = 128


precise = lax.Precision.HIGHEST


def expand_mask(local_tile, block_mask):
    row_count, col_count = local_tile.shape
    row_blocks = row_count // BLOCK
    col_blocks = col_count // BLOCK
    row_start = lax.axis_index("row") * row_blocks
    col_start = lax.axis_index("col") * col_blocks
    window = lax.dynamic_slice(block_mask, (row_start, col_start), (row_blocks, col_blocks)).astype(
        jnp.float32
    )
    shaped = local_tile.reshape(row_blocks, BLOCK, col_blocks, BLOCK) * window[:, None, :, None]
    return shaped.reshape(row_count, col_count)


def matmul(left, right):
    return jnp.dot(left, right, precision=precise, preferred_element_type=jnp.float32)


def per_device(density, response, density_mask, response_mask, branch):
    masked_density = expand_mask(density, density_mask)
    masked_response = expand_mask(response, response_mask)
    column_density, column_response = (
        lax.all_gather(masked_density, "row", axis=0, tiled=True),
        lax.all_gather(masked_response, "row", axis=0, tiled=True),
    )
    segments = (
        lax.all_gather(masked_density, "col", axis=1, tiled=True),
        lax.all_gather(masked_response, "col", axis=1, tiled=True),
    )
    square = matmul(segments[0], column_density)
    product = matmul(segments[0], column_response)
    reversed_tile = matmul(segments[1], column_density)
    combined = product + reversed_tile
    local_blocks = density.shape[0] // BLOCK
    block_start = lax.axis_index("row") * local_blocks
    local_branch = lax.dynamic_slice_in_dim(branch, block_start, local_blocks, 0)
    chosen = jnp.repeat(local_branch, BLOCK)[:, None]
    new_density = jnp.where(chosen == 0, square, 2.0 * masked_density - square)
    new_response = jnp.where(chosen == 0, combined, 2.0 * masked_response - combined)
    return (new_density, new_response)


def solution(mesh):
    return jax.shard_map(
        per_device,
        mesh=mesh,
        in_specs=(P("row", "col"), P("row", "col"), P(), P(), P()),
        out_specs=(P("row", "col"), P("row", "col")),
        check_vma=False,
    )
```

profile of v0, /device:TPU:0, one launch (start us, length us, event | category | flops | bytes accessed | tf_op | source)
XLA Modules:
  0.0 1129.4 jit_solution(15626196946147196228)
XLA Ops:
  7.2 0.0 all-gather.9.cloned.1.call-start
  7.2 0.0 copy-start
  7.2 1.0 dynamic-slice_convert_fusion
  8.2 0.5 mul.43
  8.7 0.9 copy-done
  9.6 3.6 bitcast_multiply_fusion
  13.2 0.0 all-gather.9.cloned.1.call-update
  13.2 0.0 all-gather.5.cloned.1.call-start
  13.3 0.0 copy-start.1
  13.3 0.5 mul.39
  13.8 1.9 copy-done.1
  15.6 3.7 bitcast_multiply_fusion.1
  19.3 0.0 all-gather.5.cloned.1.call-update
  19.3 0.0 copy-start.2
  19.3 0.0 all-gather.7.cloned.1.call-start
  19.4 0.7 all-gather.7.cloned.1.call-update
  20.1 0.0 all-gather.11.cloned.1.call-start
  20.1 0.5 all-gather.11.cloned.1.call-update
  20.6 0.0 copy-done.2
  20.6 0.1 dynamic-slice_compare_fusion
  20.7 0.1 broadcast_bitcast_fusion
  20.8 171.2 %all-gather.9.cloned.1.call-done = f32[6144,768]{1,0:T(8,128)} async-done(((f32[1536,768]{1,0:T(8,128)}), f32[6144,768]{1,0:T(8,128)}) %all-gather.9.cloned.1.call-update) | async-done | bytes 18874384 | tf_op jit(solution)/shard_map/all_gather | solution.py:34
  192.0 326.8 %all-gather.5.cloned.1.call-done = f32[1536,6144]{1,0:T(8,128)} async-done(((f32[1536,768]{1,0:T(8,128)}), f32[1536,6144]{1,0:T(8,128)}) %all-gather.5.cloned.1.call-update) | async-done | bytes 37748752 | tf_op jit(solution)/shard_map/all_gather | solution.py:37
  518.8 99.9 %fusion = f32[1536,768]{1,0:T(8,128)} fusion(f32[1536,6144]{1,0:T(8,128)} %all-gather.5.cloned.1.call-done, f32[6144,768]{1,0:T(8,128)} %all-gather.9.cloned.1.call-done), kind=kOutput, calls=%fused_computation.8 | convolution fusion | flops 86973087744 | bytes 61341696 | tf_op jit(solution)/shard_map/dot_general | solution.py:26
  618.6 77.4 %all-gather.7.cloned.1.call-done = f32[6144,768]{1,0:T(8,128)} async-done(((f32[1536,768]{1,0:T(8,128)}), f32[6144,768]{1,0:T(8,128)}) %all-gather.7.cloned.1.call-update) | async-done | bytes 18874384 | tf_op jit(solution)/shard_map/all_gather | solution.py:33
  696.0 100.3 %subtract_select_fusion.1 = f32[1536,768]{1,0:T(8,128)} fusion(f32[1536,768]{1,0:T(8,128)} %bitcast_multiply_fusion.1, pred[1536]{0:T(1024)(128)(4,1)S(1)} %broadcast_bitcast_fusion, f32[1536,6144]{1,0:T(8,128)} %all-gather.5.cloned.1.call-done, f32[6144,768]{1,0:T(8,128)} %all-gather.7.cloned.1.call-done), kind=kOutput, calls=%fused_computation.1 | convolution fusion | flops 86976626688 | bytes 66061824 | tf_op jit(solution)/shard_map/dot_general | solution.py:26
  796.3 225.8 %all-gather.11.cloned.1.call-done = f32[1536,6144]{1,0:T(8,128)} async-done(((f32[1536,768]{1,0:T(8,128)}), f32[1536,6144]{1,0:T(8,128)}) %all-gather.11.cloned.1.call-update) | async-done | bytes 37748752 | tf_op jit(solution)/shard_map/all_gather | solution.py:38
  1022.1 100.8 %subtract_select_fusion = f32[1536,768]{1,0:T(8,128)} fusion(f32[1536,768]{1,0:T(8,128)} %bitcast_multiply_fusion, f32[1536,768]{1,0:T(8,128)} %fusion, f32[1536,6144]{1,0:T(8,128)} %all-gather.11.cloned.1.call-done, f32[6144,768]{1,0:T(8,128)} %all-gather.7.cloned.1.call-done, pred[1536]{0:T(1024)(128)(4,1)S(1)} %broadcast_bitcast_fusion), kind=kOutput, calls=%fused_computation | convolution fusion | flops 86977806336 | bytes 70780416 | tf_op jit(solution)/shard_map/dot_general | solution.py:26
Async XLA Ops:
  7.2 184.9 %all-gather.9.cloned.1.call-start = ((), (), s32[]{:S(2)}) async-start(), calls=%async_computation.2 | async-start | bytes 23592960 | tf_op jit(solution)/shard_map/all_gather | solution.py:34
  7.2 2.4 copy-start
  13.2 505.5 %all-gather.5.cloned.1.call-start = ((), (), s32[]{:S(2)}) async-start(), calls=%async_computation | async-start | bytes 42467328 | tf_op jit(solution)/shard_map/all_gather | solution.py:37
  13.3 2.3 copy-start.1
  19.3 1.3 copy-start.2
  19.3 676.7 %all-gather.7.cloned.1.call-start = ((), (), s32[]{:S(2)}) async-start(), calls=%async_computation.1 | async-start | bytes 23592960 | tf_op jit(solution)/shard_map/all_gather | solution.py:33
  20.1 1002.0 %all-gather.11.cloned.1.call-start = ((), (), s32[]{:S(2)}) async-start(), calls=%async_computation.3 | async-start | bytes 42467328 | tf_op jit(solution)/shard_map/all_gather | solution.py:38
Sparse Core Ops, SparseCore 0:
  13.4 178.6 all-gather.8
  194.2 324.5 all-gather.4
  521.2 174.7 all-gather.6
  697.5 324.5 all-gather.10
where the time goes:
time: 1130 us
  waiting for transfers between devices  802 us (71%)
  matrix products  301 us (27%)
  between operations  13.8 us (1%)
    all_gather x1, waiting for transfers between devices, per_device(): lax.all_gather(masked_density, 'col', axis=1, tiled=True)  327 us
    dot_general x3, matrix products, matmul(): jnp.dot(left, right, precision=precise, preferred_element_type=jnp.float32)  301 us
    all_gather x1, waiting for transfers between devices, per_device(): lax.all_gather(masked_response, 'col', axis=1, tiled=True)  226 us
    all_gather x1, waiting for transfers between devices, per_device(): lax.all_gather(masked_response, 'row', axis=0, tiled=True)  171 us
    all_gather x1, waiting for transfers between devices, per_device(): lax.all_gather(masked_density, 'row', axis=0, tiled=True)  77.4 us
  transfers between devices with their start and end apart: 4, of which 4 were waited for; matrix products, arithmetic and copies ran while one was open for 18% of the time, Pallas kernels for 0%

commit v1 on v0

--- a/solution.py
+++ b/solution.py
@@ -1,12 +1,19 @@
+import functools
+
 import jax
 import jax.numpy as jnp
 from jax import lax
+from jax.experimental import pallas as pl
+from jax.experimental.pallas import tpu as pltpu
 from jax.sharding import PartitionSpec as P
 
 BLOCK = 128
-
-
-precise = lax.Precision.HIGHEST
+CORES = 2
+SHARES = ((5, 8), (3, 4))
+VMEM = 60 * 2**20
+
+
+precise = lax.Precision.HIGH
 
 
 def expand_mask(local_tile, block_mask):
@@ -26,21 +33,227 @@
     return jnp.dot(left, right, precision=precise, preferred_element_type=jnp.float32)
 
 
+def whole_products(masked_density, masked_response):
+    column_density, column_response = (
+        lax.all_gather(masked_density, "row", axis=0, tiled=True),
+        lax.all_gather(masked_response, "row", axis=0, tiled=True),
+    )
+    segments = (
+        lax.all_gather(masked_density, "col", axis=1, tiled=True),
+        lax.all_gather(masked_response, "col", axis=1, tiled=True),
+    )
+    square = matmul(segments[0], column_density)
+    product = matmul(segments[0], column_response)
+    reversed_tile = matmul(segments[1], column_density)
+    return square, product + reversed_tile
+
+
+def pack_kernel(row_blocks, col_blocks, slots, density, response, packed):
+    for m, tile in enumerate((density, response)):
+
+        @pl.loop(0, row_blocks)
+        def _(i):
+            rows = pl.ds(pl.multiple_of(i * BLOCK, BLOCK), BLOCK)
+            for j in range(col_blocks):
+                slot = slots[(m * row_blocks + i) * col_blocks + j]
+
+                @pl.when(slot >= 0)
+                def _():
+                    packed[slot] = tile[rows, j * BLOCK : (j + 1) * BLOCK]
+
+
+def pack(slots, density, response, capacity):
+    rows, cols = density.shape
+    return pl.pallas_call(
+        functools.partial(pack_kernel, rows // BLOCK, cols // BLOCK),
+        grid_spec=pltpu.PrefetchScalarGridSpec(
+            num_scalar_prefetch=1,
+            grid=(1,),
+            in_specs=[pl.BlockSpec((rows, cols), lambda g, s: (0, 0))] * 2,
+            out_specs=pl.BlockSpec((capacity, BLOCK, BLOCK), lambda g, s: (0, 0, 0)),
+        ),
+        out_shape=jax.ShapeDtypeStruct((capacity, BLOCK, BLOCK), jnp.float32),
+        compiler_params=pltpu.CompilerParams(vmem_limit_bytes=VMEM),
+        name="pack_blocks",
+    )(slots, density, response)
+
+
+def split(value):
+    high = value.astype(jnp.bfloat16)
+    return high, (value - high.astype(jnp.float32)).astype(jnp.bfloat16)
+
+
+def accumulate_kernel(lhs, first, row_blocks, col_blocks, step_blocks, table, *refs):
+    bufs, columns, refs = refs[:2], refs[2:4], refs[4:]
+    before, refs = ((), refs) if first else (refs[:lhs], refs[lhs:])
+    after, (left_high, left_low, right_high, right_low) = refs[:lhs], refs[lhs:]
+    step = pl.program_id(0)
+    depth = col_blocks * BLOCK
+    width = right_high.shape[1]
+
+    @pl.when(step == 0)
+    def _():
+        for b in range(2):
+
+            @pl.loop(0, col_blocks)
+            def _(i):
+                source = pl.ds(pl.multiple_of(i * BLOCK, BLOCK), BLOCK)
+                target = pl.ds(pl.multiple_of(b * depth + i * BLOCK, BLOCK), BLOCK)
+                right_high[target, :], right_low[target, :] = split(columns[b][source, :])
+
+    for b in range(2):
+        for m in range(lhs):
+
+            @pl.loop(0, step_blocks)
+            def _(i):
+                rows = pl.ds(pl.multiple_of(i * BLOCK, BLOCK), BLOCK)
+                base = ((b * 2 + m) * row_blocks + step * step_blocks + i) * col_blocks
+                for j in range(col_blocks):
+                    slot = table[2 + base + j]
+                    cols = slice(b * depth + j * BLOCK, b * depth + (j + 1) * BLOCK)
+
+                    @pl.when(slot >= 0)
+                    def _():
+                        left_high[m, rows, cols], left_low[m, rows, cols] = split(bufs[b][slot])
+
+                    @pl.when(slot < 0)
+                    def _():
+                        empty = jnp.zeros((BLOCK, BLOCK), jnp.bfloat16)
+                        left_high[m, rows, cols] = empty
+                        left_low[m, rows, cols] = empty
+
+    tile = 2 * BLOCK if width % (2 * BLOCK) == 0 else BLOCK
+    dot = functools.partial(jnp.dot, preferred_element_type=jnp.float32)
+    for m in range(lhs):
+
+        @pl.loop(0, width // tile)
+        def _(t):
+            cols = pl.ds(pl.multiple_of(t * tile, tile), tile)
+            high, low = right_high[:, cols], right_low[:, cols]
+            total = dot(left_high[m], high) + (dot(left_high[m], low) + dot(left_low[m], high))
+            after[m][:, cols] = total if first else before[m][:, cols] + total
+
+
+def accumulate(table, bufs, column, shape, lhs, before=None):
+    rows, cols = shape
+    row_blocks, col_blocks = rows // BLOCK, cols // BLOCK
+    steps = 3 if row_blocks % 3 == 0 else 1
+    step_rows = rows // steps
+    first = before is None
+    once = pl.Buffered(1)
+    part = pl.BlockSpec((step_rows, cols), lambda g, s: (g, 0))
+    capacity = bufs[0].shape[0]
+    return pl.pallas_call(
+        functools.partial(accumulate_kernel, lhs, first, row_blocks, col_blocks, row_blocks // steps),
+        grid_spec=pltpu.PrefetchScalarGridSpec(
+            num_scalar_prefetch=1,
+            grid=(steps,),
+            in_specs=[
+                pl.BlockSpec((capacity, BLOCK, BLOCK), lambda g, s: (0, 0, 0), pipeline_mode=once)
+            ]
+            * 2
+            + [
+                pl.BlockSpec((cols, cols), lambda g, s: (s[0], 0), pipeline_mode=once),
+                pl.BlockSpec((cols, cols), lambda g, s: (s[1], 0), pipeline_mode=once),
+            ]
+            + ([] if first else [part] * lhs),
+            out_specs=[part] * lhs,
+            scratch_shapes=[pltpu.VMEM((lhs, step_rows, 2 * cols), jnp.bfloat16)] * 2
+            + [pltpu.VMEM((2 * cols, cols), jnp.bfloat16)] * 2,
+        ),
+        out_shape=[jax.ShapeDtypeStruct(shape, jnp.float32)] * lhs,
+        input_output_aliases={} if first else {5 + m: m for m in range(lhs)},
+        compiler_params=pltpu.CompilerParams(vmem_limit_bytes=VMEM),
+        cost_estimate=pl.CostEstimate(
+            flops=2 * 3 * lhs * rows * 2 * cols * cols,
+            bytes_accessed=4 * (2 * cols * cols + 2 * lhs * rows * cols) + 8 * capacity * BLOCK * BLOCK,
+            transcendentals=0,
+        ),
+        name="accumulate_blocks",
+    )(table, *bufs, column, column, *(() if first else before))
+
+
+def packed_products(capacity, density, response, masked_density, masked_response, slots):
+    shape = density.shape
+    devices = lax.axis_size("col")
+    chips = devices // CORES
+    order = [0] + list(range(1, chips, 2)) + list(range(2, chips, 2))[::-1]
+    place = [order.index(z) for z in range(chips)]
+    me = lax.axis_index("col")
+    core = lax.rem(me, CORES)
+    position = jnp.array(place, jnp.int32)[me // CORES]
+
+    def move(value, by):
+        pairs = [
+            (order[p] * CORES + k, order[(p + by) % chips] * CORES + k)
+            for p in range(chips)
+            for k in range(CORES)
+        ]
+        return lax.ppermute(value, "col", pairs)
+
+    def swap(value):
+        return lax.ppermute(value, "col", [(d, d ^ 1) for d in range(devices)])
+
+    column_density = lax.all_gather(masked_density, "row", axis=0, tiled=True)
+    column_response = lax.all_gather(masked_response, "row", axis=0, tiled=True)
+
+    mine = lax.dynamic_index_in_dim(slots, me, 0, keepdims=False)
+    own = pack(mine, density, response, capacity)
+    def paired(value, offset):
+        chip = jnp.array(order, jnp.int32)[lax.rem(position + offset + chips, chips)]
+        ids = [chip * CORES + core, chip * CORES + 1 - core]
+        tables = [lax.dynamic_index_in_dim(slots, i, 0, keepdims=False) for i in ids]
+        return jnp.concatenate([jnp.stack(ids), *tables]), (value, swap(value))
+
+    pairs = [paired(own, 0)]
+    ahead = behind = own
+    for step in range(1, (chips + 1) // 2):
+        ahead, behind = move(ahead, 1), move(behind, -1)
+        pairs += [paired(ahead, -step), paired(behind, step)]
+    last = ()
+    if chips % 2 == 0:
+        half = capacity // 2
+        last = (move(ahead[:half], 1), move(behind[half:], -1))
+
+    total = None
+    for table, bufs in pairs:
+        total = accumulate(table, bufs, column_density, shape, 2, total)
+    if last:
+        last, total = lax.optimization_barrier((last, total))
+        pairs.append(paired(jnp.concatenate(last), chips // 2))
+        total = accumulate(*pairs[-1], column_density, shape, 2, total)
+    square, combined = total
+    for table, bufs in pairs:
+        (combined,) = accumulate(table, bufs, column_response, shape, 1, [combined])
+    return square, combined
+
+
 def per_device(density, response, density_mask, response_mask, branch):
     masked_density = expand_mask(density, density_mask)
     masked_response = expand_mask(response, response_mask)
-    column_density, column_response = (
-        lax.all_gather(masked_density, "row", axis=0, tiled=True),
-        lax.all_gather(masked_response, "row", axis=0, tiled=True),
-    )
-    segments = (
-        lax.all_gather(masked_density, "col", axis=1, tiled=True),
-        lax.all_gather(masked_response, "col", axis=1, tiled=True),
-    )
-    square = matmul(segments[0], column_density)
-    product = matmul(segments[0], column_response)
-    reversed_tile = matmul(segments[1], column_density)
-    combined = product + reversed_tile
+
+    rows, cols = lax.axis_size("row"), lax.axis_size("col")
+    row_blocks, col_blocks = density.shape[0] // BLOCK, density.shape[1] // BLOCK
+    occupied = jnp.stack([density_mask, response_mask]).reshape(2, rows, row_blocks, cols, col_blocks)
+    occupied = occupied.transpose(1, 3, 0, 2, 4).reshape(rows, cols, -1)
+    fullest = jnp.max(jnp.sum(occupied, axis=-1))
+    line = lax.dynamic_index_in_dim(occupied, lax.axis_index("row"), 0, keepdims=False)
+    slots = jnp.where(line > 0, jnp.cumsum(line, axis=-1) - 1, -1).astype(jnp.int32)
+
+    blocks = occupied.shape[-1]
+    capacities = [blocks * share[0] // share[1] // 2 * 2 for share in SHARES]
+    level = sum((fullest > capacity).astype(jnp.int32) for capacity in capacities)
+    square, combined = lax.switch(
+        level,
+        [functools.partial(packed_products, capacity) for capacity in capacities]
+        + [lambda d, r, md, mr, s: whole_products(md, mr)],
+        density,
+        response,
+        masked_density,
+        masked_response,
+        slots,
+    )
+
     local_blocks = density.shape[0] // BLOCK
     block_start = lax.axis_index("row") * local_blocks
     local_branch = lax.dynamic_slice_in_dim(branch, block_start, local_blocks, 0)

time: 1130 us -> 622 us (0.55)
  waiting for transfers between devices: 802 us -> 264 us
  matrix products: 301 us -> 0 us
  Pallas kernels: 0 us -> 276 us
  local copies, waits for them, and re-layouts: 3.8 us -> 18.9 us
  other arithmetic: 8.32 us -> 23 us
    all_gather x4 -> x2, waiting for transfers between devices: 801 us -> 0.01 us  [the longest x1 0.01 us: packed_products(): column_density = lax.all_gather(masked_density, 'row', axis=0, tiled=True)]
    dot_general x3 -> x0, matrix products: 301 us -> none  [matmul(): jnp.dot(left, right, precision=precise, preferred_element_type=jnp.float32)]
    pallas_call x0 -> x9, Pallas kernels: none -> 276 us  [the longest x8 266 us: accumulate(): pl.pallas_call(functools.partial(accumulate_kernel, lhs, first, row_block...]
    ppermute x0 -> x8, waiting for transfers between devices: none -> 262 us  [the longest x4 253 us: move(): return lax.ppermute(value, 'col', pairs)]
  transfers between devices with their start and end apart: 4 -> 10, of which waited for: 4 -> 3; matrix products, arithmetic and copies ran while one was open for 18% -> 2% of each run, Pallas kernels for 0% -> 29%
where the time goes in v1:
time: 622 us; the launch traced here: 616 us
  Pallas kernels  276 us (44%)
  waiting for transfers between devices  264 us (42%)
  other arithmetic  23 us (4%)
  local copies, waits for them, and re-layouts  18.9 us (3%)
  between operations  15.7 us (3%)
  loops' own time  10.6 us (2%)
  starting transfers between devices  8.24 us (1%)
    pallas_call x8, Pallas kernels, accumulate(): pl.pallas_call(functools.partial(accumulate_kernel, lhs, first, row_block...  266 us
    ppermute x4, waiting for transfers between devices, move(): return lax.ppermute(value, 'col', pairs)  253 us
  transfers between devices with their start and end apart: 10, of which 3 were waited for; matrix products, arithmetic and copies ran while one was open for 2% of the time, Pallas kernels for 29%

profile of v1, /device:TPU:0, one launch (start us, length us, event | category | flops | bytes accessed | tf_op | source)
XLA Modules:
  0.0 616.2 jit_solution(7120713753293749421)
XLA Ops:
  7.2 0.8 copy.44
  8.0 0.1 stack.58
  8.1 0.8 copy.43
  8.9 0.1 stack.57
  9.0 0.2 fusion.2
  9.3 0.6 reduce_max.9
  11.3 0.5 copy.45
  11.8 0.2 reshape.71
  12.0 1.0 dynamic-slice_convert_fusion
  13.0 0.5 mul.95
  13.5 0.9 copy-done
  14.4 3.7 bitcast_multiply_fusion.1
  18.1 0.5 mul.98
  18.6 3.7 bitcast_multiply_fusion
  22.3 0.6 reduce-window.6
  22.8 0.2 slice_reduce_fusion
  23.1 574.8 %conditional.1 = (f32[1536,768]{1,0:T(8,128)}, f32[1536,768]{1,0:T(8,128)}) conditional(s32[]{:T(128)} %clamp.3, ((), (), s32[8,144]{1,0:T(8,128)S(1)}, f32[1536,768]{1,0:T(8,128)}, f32[1536,768]{1,0:T(8,128)}, /*index=5*/(), f32[1536,768]{1,0:T(8,128)}, (), (), f32[1536,768]{1,0:T(8,128)}, /*index=10*/s32[8,2,128]{2,0,1:T(8,128)S(1)}, ...), branch_computations={%region_4.5_spmd, %region_5.6_spmd, %region_6.7_spmd} | conditional | flops 130460811264 | bytes 660654656 | solution.py:246
  23.1 0.7 all-gather.9.cloned.1.call-update
  23.9 0.7 all-gather.11.cloned.1.call-update
  24.6 0.7 dynamic_slice.66
  28.1 0.7 fusion.3
  31.5 0.6 constant_dynamic-slice_fusion.1
  32.1 10.0 %pack_blocks.2.refs_0_ = f32[90,128,128]{2,1,0:T(8,128)} custom-call(s32[144]{0:T(256)} %bitcast.86, f32[1536,768]{1,0:T(8,128)} %get-tuple-element.47.density, f32[1536,768]{1,0:T(8,128)} %get-tuple-element.48.response), custom_call_target="tpu_custom_call" | custom-call | tf_op jit(solution)/shard_map/cond/branch_0_fun/pack_blocks/pallas_call | solution.py:67
  42.0 3.9 collective-permute-start
  45.9 1.1 collective-permute-start.2
  47.1 127.5 %collective-permute-done.refs_0_ = f32[90,128,128]{2,1,0:T(8,128)} collective-permute-done((f32[90,128,128]{2,1,0:T(8,128)}, f32[90,128,128]{2,1,0:T(8,128)}, u32[]{:S(2)}, u32[]{:S(2)}) %collective-permute-start) | collective-permute-done | bytes 5898272 | tf_op jit(solution)/shard_map/cond/branch_0_fun/ppermute | solution.py:192
  174.6 125.9 %collective-permute-done.2.refs_0_ = f32[90,128,128]{2,1,0:T(8,128)} collective-permute-done((f32[90,128,128]{2,1,0:T(8,128)}, f32[90,128,128]{2,1,0:T(8,128)}, u32[]{:S(2)}, u32[]{:S(2)}) %collective-permute-start.2) | collective-permute-done | bytes 5898272 | tf_op jit(solution)/shard_map/cond/branch_0_fun/ppermute | solution.py:192
  300.5 0.6 pad_add_fusion.3.table
  301.1 0.7 pad_add_fusion.1
  301.8 3.7 slice.29
  305.5 1.7 collective-permute-start.1
  307.2 3.8 slice.30
  311.0 1.4 collective-permute-start.3
  312.4 40.9 %accumulate_blocks.16 = (f32[1536,768]{1,0:T(8,128)}, f32[1536,768]{1,0:T(8,128)}) custom-call(s32[290]{0:T(512)} %pad_add_fusion.3.table, f32[90,128,128]{2,1,0:T(8,128)} %pack_blocks.2.refs_0_, f32[90,128,128]{2,1,0:T(8,128)} %collective-permute-done.6.refs_1_, f32[6144,768]{1,0:T(8,128)} %all-gather.9.cloned.1.call-done.refs_2_.refs_3_, ...), custom_call_target="tpu_custom_call" | custom-call | flops 21743271936 | bytes 35389440 | tf_op jit(solution)/shard_map/cond/branch_0_fun/accumulate_blocks/pallas_call | solution.py:146
  353.3 41.7 %accumulate_blocks.17 = (f32[1536,768]{1,0:T(8,128)}, f32[1536,768]{1,0:T(8,128)}) custom-call(s32[290]{0:T(512)} %get-tuple-element.144.table, f32[90,128,128]{2,1,0:T(8,128)} %collective-permute-done.refs_0_, f32[90,128,128]{2,1,0:T(8,128)} %collective-permute-done.5.refs_1_, ...), custom_call_target="tpu_custom_call", output_to_operand_aliasing={{0}: (5, {}), {1}: (6, {})} | custom-call | flops 21743271936 | bytes 35389440 | tf_op jit(solution)/shard_map/cond/branch_0_fun/accumulate_blocks/pallas_call | solution.py:146
  395.0 41.7 %accumulate_blocks.18 = (f32[1536,768]{1,0:T(8,128)}, f32[1536,768]{1,0:T(8,128)}) custom-call(s32[290]{0:T(512)} %get-tuple-element.143.table, f32[90,128,128]{2,1,0:T(8,128)} %collective-permute-done.2.refs_0_, f32[90,128,128]{2,1,0:T(8,128)} %collective-permute-done.4.refs_1_, ...), custom_call_target="tpu_custom_call", output_to_operand_aliasing={{0}: (5, {}), {1}: (6, {})} | custom-call | flops 21743271936 | bytes 35389440 | tf_op jit(solution)/shard_map/cond/branch_0_fun/accumulate_blocks/pallas_call | solution.py:146
  436.8 0.2 constant_dynamic-update-slice_fusion.1
  437.0 2.0 constant_dynamic-update-slice_fusion.refs_0_
  439.0 2.5 copy-done.2
  441.5 0.6 pad_add_fusion.table
  442.2 9.1 %collective-permute-done.7.refs_1_ = f32[90,128,128]{2,1,0:T(8,128)} collective-permute-done((f32[90,128,128]{2,1,0:T(8,128)S(1)}, f32[90,128,128]{2,1,0:T(8,128)}, u32[]{:S(2)}, u32[]{:S(2)}) %collective-permute-start.7) | collective-permute-done | bytes 5898272 | tf_op jit(solution)/shard_map/cond/branch_0_fun/ppermute | solution.py:195
  451.2 41.8 %accumulate_blocks.19 = (f32[1536,768]{1,0:T(8,128)}, f32[1536,768]{1,0:T(8,128)}) custom-call(s32[290]{0:T(512)} %pad_add_fusion.table, f32[90,128,128]{2,1,0:T(8,128)} %copy-done.2, f32[90,128,128]{2,1,0:T(8,128)} %collective-permute-done.7.refs_1_, ...), custom_call_target="tpu_custom_call", output_to_operand_aliasing={{0}: (5, {}), {1}: (6, {})} | custom-call | flops 21743271936 | bytes 35389440 | tf_op jit(solution)/shard_map/cond/branch_0_fun/accumulate_blocks/pallas_call | solution.py:146
  493.0 24.8 %accumulate_blocks.20.refs_4_ = f32[1536,768]{1,0:T(8,128)} custom-call(s32[290]{0:T(512)} %pad_add_fusion.3.table, f32[90,128,128]{2,1,0:T(8,128)} %pack_blocks.2.refs_0_, f32[90,128,128]{2,1,0:T(8,128)} %collective-permute-done.6.refs_1_, f32[6144,768]{1,0:T(8,128)} %all-gather.11.cloned.1.call-done.refs_2_.refs_3_, ...), custom_call_target="tpu_custom_call", output_to_operand_aliasing={{}: (5, {})} | custom-call | flops 10871635968 | bytes 25952256 | tf_op jit(solution)/shard_map/cond/branch_0_fun/accumulate_blocks/pallas_call | solution.py:146
  517.9 25.2 %accumulate_blocks.21.refs_4_ = f32[1536,768]{1,0:T(8,128)} custom-call(s32[290]{0:T(512)} %get-tuple-element.144.table, f32[90,128,128]{2,1,0:T(8,128)} %collective-permute-done.refs_0_, f32[90,128,128]{2,1,0:T(8,128)} %collective-permute-done.5.refs_1_, f32[6144,768]{1,0:T(8,128)} %all-gather.11.cloned.1.call-done.refs_2_.refs_3_, ...), custom_call_target="tpu_custom_call", output_to_operand_aliasing={{}: (5, {})} | custom-call | flops 10871635968 | bytes 25952256 | tf_op jit(solution)/shard_map/cond/branch_0_fun/accumulate_blocks/pallas_call | solution.py:146
  543.1 24.8 %accumulate_blocks.22.refs_4_ = f32[1536,768]{1,0:T(8,128)} custom-call(s32[290]{0:T(512)} %get-tuple-element.143.table, f32[90,128,128]{2,1,0:T(8,128)} %collective-permute-done.2.refs_0_, f32[90,128,128]{2,1,0:T(8,128)} %collective-permute-done.4.refs_1_, ...), custom_call_target="tpu_custom_call", output_to_operand_aliasing={{}: (5, {})} | custom-call | flops 10871635968 | bytes 25952256 | tf_op jit(solution)/shard_map/cond/branch_0_fun/accumulate_blocks/pallas_call | solution.py:146
  568.0 24.8 %accumulate_blocks.23 = f32[1536,768]{1,0:T(8,128)} custom-call(s32[290]{0:T(512)} %pad_add_fusion.table, f32[90,128,128]{2,1,0:T(8,128)} %copy-done.2, f32[90,128,128]{2,1,0:T(8,128)} %collective-permute-done.7.refs_1_, f32[6144,768]{1,0:T(8,128)} %all-gather.11.cloned.1.call-done.refs_2_.refs_3_, ...), custom_call_target="tpu_custom_call", output_to_operand_aliasing={{}: (5, {})} | custom-call | flops 10871635968 | bytes 25952256 | tf_op jit(solution)/shard_map/cond/branch_0_fun/accumulate_blocks/pallas_call | solution.py:146
  597.9 0.1 dynamic-slice_compare_fusion
  598.0 11.1 %subtract_select_fusion = (f32[1536,768]{1,0:T(8,128)}, f32[1536,768]{1,0:T(8,128)}) fusion(f32[1536,768]{1,0:T(8,128)} %get-tuple-element.95, f32[1536,768]{1,0:T(8,128)} %bitcast_multiply_fusion, pred[1536]{0:T(1024)(128)(4,1)S(1)} %broadcast_bitcast_fusion, f32[1536,768]{1,0:T(8,128)} %get-tuple-element.94, f32[1536,768]{1,0:T(8,128)} %bitcast_multiply_fusion.1), kind=kLoop, calls=%fused_computation.37 | loop fusion | flops 7077888 | bytes 28313088 | tf_op jit(solution)/shard_map/jit(_where)/select_n | solution.py:262
  (32 shorter events, 0.4 us)
Async XLA Ops:
  12.0 2.4 copy-start
  13.5 5.1 slice-start
  14.4 4.2 slice-start.1
  23.1 574.8 %copy-start.5 = (s32[48]{0:T(128)S(1)}, s32[48]{0:T(128)}, u32[]{:S(2)}) copy-start(s32[48]{0:T(128)} %param.22) | copy-start | bytes 580
  23.1 289.3 %all-gather.9.cloned.1.call-start = ((), (), s32[]{:S(2)}) async-start(), calls=%async_computation | async-start | bytes 23592960 | tf_op jit(solution)/shard_map/cond/branch_0_fun/all_gather | solution.py:197
  23.1 1.5 copy-start.3
  23.8 469.2 %all-gather.11.cloned.1.call-start = ((), (), s32[]{:S(2)}) async-start(), calls=%async_computation.1 | async-start | bytes 23592960 | tf_op jit(solution)/shard_map/cond/branch_0_fun/all_gather | solution.py:198
  42.0 132.5 %collective-permute-start = (f32[90,128,128]{2,1,0:T(8,128)}, f32[90,128,128]{2,1,0:T(8,128)}, u32[]{:S(2)}, u32[]{:S(2)}) collective-permute-start(f32[90,128,128]{2,1,0:T(8,128)} %pack_blocks.2.refs_0_), channel_id=1, source_target_pairs={{0,2},{1,3},{2,6},{3,7},{6,4},{7,5},{4,0},{5,1},{8,10},{9,11},{10,... | collective-permute-start | bytes 17694728 | tf_op jit(solution)/shard_map/cond/branch_0_fun/ppermute | solution.py:192
  45.9 254.5 %collective-permute-start.2 = (f32[90,128,128]{2,1,0:T(8,128)}, f32[90,128,128]{2,1,0:T(8,128)}, u32[]{:S(2)}, u32[]{:S(2)}) collective-permute-start(f32[90,128,128]{2,1,0:T(8,128)} %pack_blocks.2.refs_0_), channel_id=1, source_target_pairs={{0,4},{1,5},{2,0},{3,1},{6,2},{7,3},{4,6},{5,7},{8,12},{9,13},{10,... | collective-permute-start | bytes 17694728 | tf_op jit(solution)/shard_map/cond/branch_0_fun/ppermute | solution.py:192
  47.1 265.3 %collective-permute-start.6 = (f32[90,128,128]{2,1,0:T(8,128)}, f32[90,128,128]{2,1,0:T(8,128)}, u32[]{:S(2)}, u32[]{:S(2)}) collective-permute-start(f32[90,128,128]{2,1,0:T(8,128)} %pack_blocks.2.refs_0_), channel_id=1, source_target_pairs={{0,1},{1,0},{2,3},{3,2},{4,5},{5,4},{6,7},{7,6},{8,9},{9,8},{10,11... | collective-permute-start | bytes 17694728 | tf_op jit(solution)/shard_map/cond/branch_0_fun/ppermute | solution.py:195
  174.6 178.7 %collective-permute-start.5 = (f32[90,128,128]{2,1,0:T(8,128)}, f32[90,128,128]{2,1,0:T(8,128)}, u32[]{:S(2)}, u32[]{:S(2)}) collective-permute-start(f32[90,128,128]{2,1,0:T(8,128)} %collective-permute-done.refs_0_), channel_id=1, source_target_pairs={{0,1},{1,0},{2,3},{3,2},{4,5},{5,4},{6,7},{7,6},{8,9},{9,8},{10,11... | collective-permute-start | bytes 17694728 | tf_op jit(solution)/shard_map/cond/branch_0_fun/ppermute | solution.py:195
  300.4 94.6 %collective-permute-start.4 = (f32[90,128,128]{2,1,0:T(8,128)}, f32[90,128,128]{2,1,0:T(8,128)}, u32[]{:S(2)}, u32[]{:S(2)}) collective-permute-start(f32[90,128,128]{2,1,0:T(8,128)} %collective-permute-done.2.refs_0_), channel_id=1, source_target_pairs={{0,1},{1,0},{2,3},{3,2},{4,5},{5,4},{6,7},{7,6},{8,9},{9,8},{10,11... | collective-permute-start | bytes 17694728 | tf_op jit(solution)/shard_map/cond/branch_0_fun/ppermute | solution.py:195
  305.5 131.2 %collective-permute-start.1 = (f32[45,128,128]{2,1,0:T(8,128)}, f32[45,128,128]{2,1,0:T(8,128)S(1)}, u32[]{:S(2)}, u32[]{:S(2)}) collective-permute-start(f32[45,128,128]{2,1,0:T(8,128)} %slice.29), channel_id=1, source_target_pairs={{0,2},{1,3},{2,6},{3,7},{6,4},{7,5},{4,0},{5,1},{8,10},{9,11},{10,... | collective-permute-start | bytes 8847368 | tf_op jit(solution)/shard_map/cond/branch_0_fun/ppermute | solution.py:192
  311.0 125.7 %collective-permute-start.3 = (f32[45,128,128]{2,1,0:T(8,128)}, f32[45,128,128]{2,1,0:T(8,128)}, u32[]{:S(2)}, u32[]{:S(2)}) collective-permute-start(f32[45,128,128]{2,1,0:T(8,128)} %slice.30), channel_id=1, source_target_pairs={{0,4},{1,5},{2,0},{3,1},{6,2},{7,3},{4,6},{5,7},{8,12},{9,13},{10,... | collective-permute-start | bytes 8847368 | tf_op jit(solution)/shard_map/cond/branch_0_fun/ppermute | solution.py:192
  439.0 2.5 copy-start.2
  441.5 9.7 %collective-permute-start.7 = (f32[90,128,128]{2,1,0:T(8,128)S(1)}, f32[90,128,128]{2,1,0:T(8,128)}, u32[]{:S(2)}, u32[]{:S(2)}) collective-permute-start(f32[90,128,128]{2,1,0:T(8,128)S(1)} %constant_dynamic-update-slice_fusion.refs_0_), channel_id=1, source_target_pairs={{0,1},{1,0},{2,3},{3,2},{4,5},{5,4},{6,7},{7,6},{8,9},{9,8},{10,11... | collective-permute-start | bytes 17694728 | tf_op jit(solution)/shard_map/cond/branch_0_fun/ppermute | solution.py:195
Sparse Core Ops, SparseCore 0:
  26.4 178.6 all-gather.8
  207.5 175.9 all-gather.10
